TPU v7x, 512 devices: a whole 4x4x16 slice. The times are simulated.
512 devices in a mesh: ctx: 64 (over z, y), ch: 8 (over x, core).
Axes of the slice: x: 4, y: 4, z: 16, core: 2. Of those that a mesh axis runs over, the one named last changes fastest.
Arguments:
- query_gate: bfloat16 [8192, 8192], P('ctx', 'ch'), may hold values from -6 to 6
- key_gate: bfloat16 [8192, 8192], P('ctx', 'ch'), may hold values from -6 to 6
- value_branch: bfloat16 [8192, 8192], P('ctx', 'ch'), may hold values from -6 to 6
- grad_out: bfloat16 [8192, 8192], P('ctx', 'ch'), may hold values from -0.625 to 0.625
- filters: float32 [512, 8192], P('ch', 'ctx'), may hold values from -2 to 2
- skip_bias: float32 [8192], P('ch'), may hold values from -2 to 2
Outputs:
- grad_query: bfloat16 [8192, 8192], P('ctx', 'ch')
- grad_key: bfloat16 [8192, 8192], P('ctx', 'ch')
- grad_value: bfloat16 [8192, 8192], P('ctx', 'ch')
- grad_filters: float32 [512, 8192], P('ch', 'ctx')
- grad_bias: float32 [8192], P('ch')
All inputs are finite; a program needn't handle non-finite values.
Results may differ from a plain program's by a relative error of at most 0.0057.
Values may be sent and summed in bfloat16 or wider, within the bound.
No kernel may reach another device: no remote copies, remote signals or barrier semaphores. Data moves between devices by JAX's collectives and lax.ppermute only.
A program may use at most 64 MiB of HBM per device.

v0:
```python
import math

import jax
import jax.numpy as jnp
from jax import lax
from jax.sharding import PartitionSpec as P

HIGHEST = lax.Precision.HIGHEST
TRIPLE_PASS_MODE = lax.Precision.HIGH


def fourier_tables(first_index, second_index, period):
    phases = first_index[:, None] * second_index[None, :] % period
    angles = phases.astype(jnp.float32) * (2.0 * math.pi / period)
    return (jnp.cos(angles), jnp.sin(angles))


def block_spectra(signal, block_count):
    channels, length = signal.shape
    block_length = length // block_count
    period = 2 * block_length
    cosine_table, sinusoid_values = fourier_tables(
        jnp.arange(block_length, dtype=jnp.int32), jnp.arange(period, dtype=jnp.int32), period
    )
    filter_parts = signal.reshape(channels, block_count, block_length)
    spectrum_real = jnp.einsum(
        "ahg,gi->ahi",
        filter_parts,
        cosine_table,
        precision=TRIPLE_PASS_MODE,
        preferred_element_type=jnp.float32,
    )
    spectrum_imaginary = -jnp.einsum(
        "ahg,gi->ahi",
        filter_parts,
        sinusoid_values,
        precision=TRIPLE_PASS_MODE,
        preferred_element_type=jnp.float32,
    )
    return (spectrum_real, spectrum_imaginary)


def segment_spectra(kernel, block_count):
    groups, length = kernel.shape
    block_length = length // block_count
    period = 2 * block_length
    cosine_table, sinusoid_values = fourier_tables(
        jnp.arange(period, dtype=jnp.int32), jnp.arange(period, dtype=jnp.int32), period
    )
    current = kernel.reshape(groups, block_count, block_length)
    previous = jnp.concatenate([jnp.zeros_like(current[:, :1]), current[:, :-1]], axis=1)

    def project(values, table):
        return jnp.einsum(
            "gpb,bn->gpn", values, table, precision=HIGHEST, preferred_element_type=jnp.float32
        )

    spectrum_real = project(previous, cosine_table[:block_length]) + project(
        current, cosine_table[block_length:]
    )
    spectrum_imaginary = -(
        project(previous, sinusoid_values[:block_length])
        + project(current, sinusoid_values[block_length:])
    )
    return (spectrum_real, spectrum_imaginary)


def across_blocks(values_real, values_imaginary):
    block_count = values_real.shape[1]
    double = 2 * block_count
    cosine_table, sinusoid_values = fourier_tables(
        jnp.arange(block_count, dtype=jnp.int32), jnp.arange(double, dtype=jnp.int32), double
    )

    def mixing(values, table):
        return jnp.einsum(
            "xjn,jm->xmn", values, table, precision=HIGHEST, preferred_element_type=jnp.float32
        )

    out_real = mixing(values_real, cosine_table) + mixing(values_imaginary, sinusoid_values)
    out_imaginary = mixing(values_imaginary, cosine_table) - mixing(values_real, sinusoid_values)
    return (out_real, out_imaginary)


def back_blocks(values_real, values_imaginary):
    double = values_real.shape[1]
    block_count = double // 2
    cosine_table, sinusoid_values = fourier_tables(
        jnp.arange(double, dtype=jnp.int32), jnp.arange(block_count, dtype=jnp.int32), double
    )

    def mixing(values, table):
        return jnp.einsum(
            "xmn,mj->xjn", values, table, precision=HIGHEST, preferred_element_type=jnp.float32
        )

    out_real = (
        mixing(values_real, cosine_table) - mixing(values_imaginary, sinusoid_values)
    ) / double
    out_imaginary = (
        mixing(values_imaginary, cosine_table) + mixing(values_real, sinusoid_values)
    ) / double
    return (out_real, out_imaginary)


def real_inverse(values_real, values_imaginary, token_positions):
    period = values_real.shape[2]
    cosine_table, sinusoid_values = fourier_tables(
        jnp.arange(period, dtype=jnp.int32), token_positions, period
    )
    first_term = jnp.einsum(
        "xpn,nk->xpk",
        values_real,
        cosine_table,
        precision=HIGHEST,
        preferred_element_type=jnp.float32,
    )
    second_term = jnp.einsum(
        "xpn,nk->xpk",
        values_imaginary,
        sinusoid_values,
        precision=HIGHEST,
        preferred_element_type=jnp.float32,
    )
    return (first_term - second_term) / period


def sequence_pass(gated, scaled, kernel, skip_row, block_count):
    channels, length = gated.shape
    groups = kernel.shape[0]
    per_group = channels // groups
    block_length = length // block_count
    period = 2 * block_length
    double = 2 * block_count
    first_real, first_imaginary = block_spectra(gated, block_count)
    gate_real, gate_imaginary = across_blocks(first_real, first_imaginary)
    first_real, first_imaginary = block_spectra(scaled, block_count)
    grad_real, grad_imaginary = across_blocks(first_real, first_imaginary)
    first_real, first_imaginary = segment_spectra(kernel, block_count)
    filter_real, filter_imaginary = across_blocks(first_real, first_imaginary)
    grouped_shape = (groups, per_group, double, period)
    gate_real = gate_real.reshape(grouped_shape)
    gate_imaginary = gate_imaginary.reshape(grouped_shape)
    grad_real = grad_real.reshape(grouped_shape)
    grad_imaginary = grad_imaginary.reshape(grouped_shape)
    filter_real = filter_real[:, None]
    filter_imaginary = filter_imaginary[:, None]
    conv_real = gate_real * filter_real - gate_imaginary * filter_imaginary
    conv_imaginary = gate_real * filter_imaginary + gate_imaginary * filter_real
    back_real = grad_real * filter_real + grad_imaginary * filter_imaginary
    back_imaginary = grad_imaginary * filter_real - grad_real * filter_imaginary
    lag_real = jnp.sum(grad_real * gate_real + grad_imaginary * gate_imaginary, axis=1)
    lag_imaginary = jnp.sum(grad_imaginary * gate_real - grad_real * gate_imaginary, axis=1)
    flat_shape = (channels, double, period)
    conv_real, conv_imaginary = back_blocks(
        conv_real.reshape(flat_shape), conv_imaginary.reshape(flat_shape)
    )
    back_real, back_imaginary = back_blocks(
        back_real.reshape(flat_shape), back_imaginary.reshape(flat_shape)
    )
    lag_real, lag_imaginary = back_blocks(lag_real, lag_imaginary)
    offsets = jnp.arange(block_length, dtype=jnp.int32)
    convolved = real_inverse(conv_real, conv_imaginary, offsets + block_length).reshape(
        channels, length
    )
    correlated = real_inverse(back_real, -back_imaginary, block_length - offsets).reshape(
        channels, length
    )
    lagged = real_inverse(lag_real, lag_imaginary, jnp.arange(period, dtype=jnp.int32))
    nearer = lagged[:, :, :block_length]
    farther = lagged[:, :, block_length:]
    farther = jnp.concatenate([farther[:, 1:], jnp.zeros_like(farther[:, :1])], axis=1)
    grad_kernel = (nearer + farther).reshape(groups, length)
    gated_wide = gated.astype(jnp.float32)
    scaled_wide = scaled.astype(jnp.float32)
    convolved = convolved + skip_row[:, None] * gated_wide
    correlated = correlated + skip_row[:, None] * scaled_wide
    grad_skip = jnp.sum(gated_wide * scaled_wide, axis=1)
    return (convolved, correlated, grad_kernel, grad_skip)


def rounded_product(first, second):
    return lax.optimization_barrier(
        (first.astype(jnp.float32) * second.astype(jnp.float32)).astype(jnp.bfloat16)
    )


def plain_product(first, second):
    return (first.astype(jnp.float32) * second.astype(jnp.float32)).astype(jnp.bfloat16)


def on_device(query_gate, key_gate, value_branch, grad_out, filters, skip_bias):
    block_count = lax.axis_size("ctx")
    kernel = lax.all_to_all(filters, "ctx", split_axis=0, concat_axis=1, tiled=True)
    channels = query_gate.shape[1] // block_count
    skip_row = lax.dynamic_slice_in_dim(skip_bias, lax.axis_index("ctx") * channels, channels)
    gated = rounded_product(key_gate, value_branch)
    scaled = rounded_product(query_gate, grad_out)
    gated_moved, scaled_moved = (
        lax.all_to_all(gated.T, "ctx", split_axis=0, concat_axis=1, tiled=True),
        lax.all_to_all(scaled.T, "ctx", split_axis=0, concat_axis=1, tiled=True),
    )
    convolved, correlated, grad_kernel, grad_skip = sequence_pass(
        gated_moved, scaled_moved, kernel, skip_row, block_count
    )
    conv_back, corr_back = (
        lax.all_to_all(
            convolved.astype(jnp.bfloat16), "ctx", split_axis=1, concat_axis=0, tiled=True
        ),
        lax.all_to_all(
            correlated.astype(jnp.bfloat16), "ctx", split_axis=1, concat_axis=0, tiled=True
        ),
    )
    conv_back = conv_back.T
    corr_back = corr_back.T
    grad_query = plain_product(grad_out, conv_back)
    grad_key = plain_product(corr_back, value_branch)
    grad_value = plain_product(corr_back, key_gate)
    grad_filters = lax.all_to_all(grad_kernel, "ctx", split_axis=1, concat_axis=0, tiled=True)
    grad_bias = lax.all_gather(grad_skip, "ctx", axis=0, tiled=True)
    return (grad_query, grad_key, grad_value, grad_filters, grad_bias)


def solution(mesh):
    in_specs = (
        P("ctx", "ch"),
        P("ctx", "ch"),
        P("ctx", "ch"),
        P("ctx", "ch"),
        P("ch", "ctx"),
        P("ch"),
    )
    out_specs = (P("ctx", "ch"), P("ctx", "ch"), P("ctx", "ch"), P("ch", "ctx"), P("ch"))
    return jax.shard_map(
        on_device, mesh=mesh, in_specs=in_specs, out_specs=out_specs, check_vma=False
    )
```

profile of v0, /device:TPU:2, one launch (start us, length us, event | category | flops | bytes accessed | tf_op | source)
XLA Modules:
  0.0 337.4 jit_solution(15547564779773200424)
XLA Ops:
  0.6 18.7 %all-to-all-start.1 = ((f32[64,1,128]{2,1,0:T(1,128)}), f32[64,1,128]{2,1,0:T(1,128)S(1)}, u32[]{:S(2)}, u32[]{:S(2)}) async-start(f32[64,1,128]{2,1,0:T(1,128)} %bitcast.201), calls=%async_computation.1 | async-start | bytes 65536 | tf_op jit(solution)/shard_map/all_to_all | solution.py:194
  25.1 8.8 %all-to-all-done.1 = f32[64,1,128]{2,1,0:T(1,128)S(1)} async-done(((f32[64,1,128]{2,1,0:T(1,128)}), f32[64,1,128]{2,1,0:T(1,128)S(1)}, u32[]{:S(2)}, u32[]{:S(2)}) %all-to-all-start.1) | async-done | bytes 32800 | tf_op jit(solution)/shard_map/all_to_all | solution.py:194
  33.9 6.5 %all-to-all-start.3 = ((bf16[64,16,128]{2,1,0:T(8,128)(2,1)}), bf16[64,16,128]{2,1,0:T(8,128)(2,1)S(1)}, u32[]{:S(2)}, u32[]{:S(2)}) async-start(bf16[64,16,128]{2,1,0:T(8,128)(2,1)} %bitcast.25), calls=%async_computation.3 | async-start | bytes 524288 | tf_op jit(solution)/shard_map/all_to_all | solution.py:201
  43.1 19.3 %all-to-all-done.3 = bf16[64,16,128]{2,1,0:T(8,128)(2,1)S(1)} async-done(((bf16[64,16,128]{2,1,0:T(8,128)(2,1)}), bf16[64,16,128]{2,1,0:T(8,128)(2,1)S(1)}, u32[]{:S(2)}, u32[]{:S(2)}) %all-to-all-start.3) | async-done | bytes 262176 | tf_op jit(solution)/shard_map/all_to_all | solution.py:201
  63.3 2.0 fusion.161
  66.2 2.0 fusion.159
  68.2 2.0 convolution_add_fusion
  70.2 2.0 convolution_subtract_fusion
  83.0 4.7 %all-to-all-start.4 = ((bf16[16,64,128]{2,0,1:T(8,128)(2,1)}), bf16[16,64,128]{2,0,1:T(8,128)(2,1)S(1)}, u32[]{:S(2)}, u32[]{:S(2)}) async-start(bf16[16,64,128]{2,0,1:T(8,128)(2,1)} %copy.29), calls=%async_computation.4 | async-start | bytes 524288 | tf_op jit(solution)/shard_map/all_to_all | solution.py:210
  91.2 18.2 %all-to-all-done.4 = bf16[16,64,128]{2,0,1:T(8,128)(2,1)S(1)} async-done(((bf16[16,64,128]{2,0,1:T(8,128)(2,1)}), bf16[16,64,128]{2,0,1:T(8,128)(2,1)S(1)}, u32[]{:S(2)}, u32[]{:S(2)}) %all-to-all-start.4) | async-done | bytes 262176 | tf_op jit(solution)/shard_map/all_to_all | solution.py:210
  109.5 2.0 fusion.70
  111.4 5.2 %all-to-all-start = ((bf16[64,16,128]{2,1,0:T(8,128)(2,1)}), bf16[64,16,128]{2,1,0:T(8,128)(2,1)S(1)}, u32[]{:S(2)}, u32[]{:S(2)}) async-start(bf16[64,16,128]{2,1,0:T(8,128)(2,1)} %bitcast.195), calls=%async_computation | async-start | bytes 524288 | tf_op jit(solution)/shard_map/all_to_all | solution.py:200
  116.6 21.4 %all-to-all-done = bf16[64,16,128]{2,1,0:T(8,128)(2,1)S(1)} async-done(((bf16[64,16,128]{2,1,0:T(8,128)(2,1)}), bf16[64,16,128]{2,1,0:T(8,128)(2,1)S(1)}, u32[]{:S(2)}, u32[]{:S(2)}) %all-to-all-start) | async-done | bytes 262176 | tf_op jit(solution)/shard_map/all_to_all | solution.py:200
  139.0 2.0 fusion.165
  141.9 2.0 fusion.163
  143.9 2.1 convolution_add_fusion.1
  146.0 2.7 subtract_reduce_fusion
  148.7 2.6 fusion.8
  151.4 2.8 fusion.10
  158.7 4.7 %all-to-all-start.5 = ((f32[1,64,128]{2,0,1:T(1,128)}), f32[1,64,128]{2,0,1:T(1,128)S(1)}, u32[]{:S(2)}, u32[]{:S(2)}) async-start(f32[1,64,128]{2,0,1:T(1,128)} %bitcast.39), calls=%async_computation.5 | async-start | bytes 65536 | tf_op jit(solution)/shard_map/all_to_all | solution.py:219
  163.4 3.7 %fusion.31 = f32[16,64,256]{2,1,0:T(8,128)S(1)} fusion(f32[64,16,256]{2,0,1:T(8,128)} %fusion.8, f32[128,16,256]{2,0,1:T(8,128)} %copy-done.4, f32[128,16,256]{2,0,1:T(8,128)S(1)} %copy-done.3, f32[128,256]{1,0:T(8,128)S(1)} %convolution_subtract_fusion.4, f32[128,256]{1,0:T(8,128)S(1)} %convolution_add_fusion.2), kind=kOutput, calls=%fused_computation.33 | convolution fusion | flops 404865024 | bytes 6553600 | tf_op jit(solution)/shard_map/xmn,mj->xjn/dot_general | solution.py:93
  172.7 5.3 %all-to-all-done.5 = f32[1,64,128]{2,0,1:T(1,128)S(1)} async-done(((f32[1,64,128]{2,0,1:T(1,128)}), f32[1,64,128]{2,0,1:T(1,128)S(1)}, u32[]{:S(2)}, u32[]{:S(2)}) %all-to-all-start.5) | async-done | bytes 32800 | tf_op jit(solution)/shard_map/all_to_all | solution.py:219
  178.0 9.8 %all-to-all-start.2 = ((bf16[16,64,128]{2,0,1:T(8,128)(2,1)}), bf16[16,64,128]{2,0,1:T(8,128)(2,1)S(1)}, u32[]{:S(2)}, u32[]{:S(2)}) async-start(bf16[16,64,128]{2,0,1:T(8,128)(2,1)} %copy.26), calls=%async_computation.2 | async-start | bytes 524288 | tf_op jit(solution)/shard_map/all_to_all | solution.py:207
  191.9 143.7 %all-reduce.2 = f32[1024]{0:T(1024)} all-reduce(f32[1024]{0:T(1024)S(1)} %dynamic-update-slice), channel_id=1, replica_groups=mesh['ctx'=64,'ch'=8] {'ctx'}, use_global_device_ids=true, to_apply=%add.2 | all-reduce | flops 1024 | bytes 8192
  (67 shorter events, 41.3 us)
Async XLA Ops:
  0.6 33.3 %all-to-all-start.1 = ((f32[64,1,128]{2,1,0:T(1,128)}), f32[64,1,128]{2,1,0:T(1,128)S(1)}, u32[]{:S(2)}, u32[]{:S(2)}) async-start(f32[64,1,128]{2,1,0:T(1,128)} %bitcast.201), calls=%async_computation.1 | async-start | bytes 65536 | tf_op jit(solution)/shard_map/all_to_all | solution.py:194
  33.9 28.5 %all-to-all-start.3 = ((bf16[64,16,128]{2,1,0:T(8,128)(2,1)}), bf16[64,16,128]{2,1,0:T(8,128)(2,1)S(1)}, u32[]{:S(2)}, u32[]{:S(2)}) async-start(bf16[64,16,128]{2,1,0:T(8,128)(2,1)} %bitcast.25), calls=%async_computation.3 | async-start | bytes 524288 | tf_op jit(solution)/shard_map/all_to_all | solution.py:201
  72.2 5.2 %copy-start = (f32[128,16,256]{2,0,1:T(8,128)}, f32[128,16,256]{2,0,1:T(8,128)S(1)}, u32[]{:S(2)}) copy-start(f32[128,16,256]{2,0,1:T(8,128)S(1)} %convolution_subtract_fusion) | copy-start | bytes 6291460
  83.0 26.5 %all-to-all-start.4 = ((bf16[16,64,128]{2,0,1:T(8,128)(2,1)}), bf16[16,64,128]{2,0,1:T(8,128)(2,1)S(1)}, u32[]{:S(2)}, u32[]{:S(2)}) async-start(bf16[16,64,128]{2,0,1:T(8,128)(2,1)} %copy.29), calls=%async_computation.4 | async-start | bytes 524288 | tf_op jit(solution)/shard_map/all_to_all | solution.py:210
  111.4 26.6 %all-to-all-start = ((bf16[64,16,128]{2,1,0:T(8,128)(2,1)}), bf16[64,16,128]{2,1,0:T(8,128)(2,1)S(1)}, u32[]{:S(2)}, u32[]{:S(2)}) async-start(bf16[64,16,128]{2,1,0:T(8,128)(2,1)} %bitcast.195), calls=%async_computation | async-start | bytes 524288 | tf_op jit(solution)/shard_map/all_to_all | solution.py:200
  143.9 2.1 copy-start.1
  146.0 5.4 %copy-start.2 = (f32[128,16,256]{2,0,1:T(8,128)}, f32[128,16,256]{2,0,1:T(8,128)S(1)}, u32[]{:S(2)}) copy-start(f32[128,16,256]{2,0,1:T(8,128)S(1)} %convolution_add_fusion.1) | copy-start | bytes 6291460
  148.7 2.7 copy-start.4
  154.1 9.3 %copy-start.3 = (f32[128,16,256]{2,0,1:T(8,128)S(1)}, f32[128,16,256]{2,0,1:T(8,128)}, u32[]{:S(2)}) copy-start(f32[128,16,256]{2,0,1:T(8,128)} %copy-done.2) | copy-start | bytes 6291460
  158.7 19.3 %all-to-all-start.5 = ((f32[1,64,128]{2,0,1:T(1,128)}), f32[1,64,128]{2,0,1:T(1,128)S(1)}, u32[]{:S(2)}, u32[]{:S(2)}) async-start(f32[1,64,128]{2,0,1:T(1,128)} %bitcast.39), calls=%async_computation.5 | async-start | bytes 65536 | tf_op jit(solution)/shard_map/all_to_all | solution.py:219
  163.4 3.7 %copy-start.5 = (f32[128,16,256]{2,0,1:T(8,128)S(1)}, f32[128,16,256]{2,0,1:T(8,128)}, u32[]{:S(2)}) copy-start(f32[128,16,256]{2,0,1:T(8,128)} %copy-done.4) | copy-start | bytes 6291460
  163.4 3.7 %copy-start.6 = (f32[64,16,256]{2,0,1:T(8,128)S(1)}, f32[64,16,256]{2,0,1:T(8,128)}, u32[]{:S(2)}) copy-start(f32[64,16,256]{2,0,1:T(8,128)} %fusion.10) | copy-start | bytes 3145732
  168.8 20.9 %copy-start.7 = (bf16[128,1024]{0,1:T(8,128)(2,1)S(1)}, bf16[128,1024]{0,1:T(8,128)(2,1)}, u32[]{:S(2)}) copy-start(bf16[128,1024]{0,1:T(8,128)(2,1)} %get-tuple-element.17) | copy-start | bytes 786436
  178.0 157.6 %all-to-all-start.2 = ((bf16[16,64,128]{2,0,1:T(8,128)(2,1)}), bf16[16,64,128]{2,0,1:T(8,128)(2,1)S(1)}, u32[]{:S(2)}, u32[]{:S(2)}) async-start(bf16[16,64,128]{2,0,1:T(8,128)(2,1)} %copy.26), calls=%async_computation.2 | async-start | bytes 524288 | tf_op jit(solution)/shard_map/all_to_all | solution.py:207
where the time goes:
time: 342 us; the launch traced here: 337 us
  blocking collectives  144 us (42%)
  waiting for transfers between devices  73 us (21%)
  matrix products  50.4 us (15%)
  starting transfers between devices  49.6 us (15%)
  local copies, waits for them, and re-layouts  13 us (4%)
  other arithmetic  5.6 us (2%)
    unnamed x1, blocking collectives  144 us
    all_to_all x1, waiting for transfers between devices, on_device(): lax.all_to_all(gated.T, 'ctx', split_axis=0, concat_axis=1, tiled=True)  21.4 us
    all_to_all x1, waiting for transfers between devices, on_device(): lax.all_to_all(scaled.T, 'ctx', split_axis=0, concat_axis=1, tiled=True)  19.3 us
    dot_general x12, matrix products, mixing(): jnp.einsum('xmn,mj->xjn', values, table, precision=HIGHEST, preferred_ele...  19 us
    all_to_all x1, starting transfers between devices, on_device(): lax.all_to_all(filters, 'ctx', split_axis=0, concat_axis=1, tiled=True)  18.7 us
    dot_general x12, matrix products, mixing(): jnp.einsum('xjn,jm->xmn', values, table, precision=HIGHEST, preferred_ele...  18.4 us
    all_to_all x1, waiting for transfers between devices, on_device(): lax.all_to_all(correlated.astype(jnp.bfloat16), 'ctx', split_axis=1, conc...  18.2 us
    unnamed x27, local copies, waits for them, and re-layouts  10.5 us
  transfers between devices with their start and end apart: 6, of which 5 were waited for; matrix products, arithmetic and copies ran while one was open for 7% of the time, Pallas kernels for 0%

commit v1 on v0

v1 whole, which is shorter than its diff:
```python
import jax
import jax.numpy as jnp
from jax import lax
from jax.experimental import pallas as pl
from jax.experimental.pallas import tpu as pltpu
from jax.sharding import PartitionSpec as P

CHANNELS = 16
EXTRA = 2 * CHANNELS
ROWS = EXTRA + 8
LANES = 128
WIDE = jnp.float32
NARROW = jnp.bfloat16


def gate_kernel(query_ref, key_ref, value_ref, grad_ref, filter_ref, out_ref):
    blocks = query_ref.shape[1] // LANES
    per_block = LANES // CHANNELS
    for block in range(blocks):
        columns = slice(block * LANES, (block + 1) * LANES)
        gated = (key_ref[:, columns].astype(WIDE) * value_ref[:, columns].astype(WIDE)).astype(NARROW)
        scaled = (query_ref[:, columns].astype(WIDE) * grad_ref[:, columns].astype(WIDE)).astype(NARROW)
        gated, scaled = gated.T, scaled.T
        for part in range(per_block):
            rows = slice(part * CHANNELS, (part + 1) * CHANNELS)
            out_ref[block * per_block + part, 0:CHANNELS, :] = gated[rows]
            out_ref[block * per_block + part, CHANNELS:EXTRA, :] = scaled[rows]
    for group in range(filter_ref.shape[0]):
        taps = jnp.broadcast_to(filter_ref[group : group + 1, :], (8, LANES))
        out_ref[group, EXTRA:ROWS, :] = taps.astype(NARROW)


def sequence_kernel(
    skip_ref, in_ref, out_ref, gated_ref, scaled_ref, taps_ref, rolled_ref, turned_ref, conv_ref, corr_ref, lag_ref
):
    count = in_ref.shape[0]
    pairs = count // 2
    height = pairs * CHANNELS
    for block in range(count):
        rows = slice(block // 2 * CHANNELS, (block // 2 + 1) * CHANNELS)
        columns = slice(block % 2 * LANES, (block % 2 + 1) * LANES)
        gated_ref[rows, columns] = in_ref[block, 0:CHANNELS, :]
        scaled_ref[rows, columns] = in_ref[block, CHANNELS:EXTRA, :]
        taps_ref[block : block + 1, :] = in_ref[block, EXTRA:ROWS, :].astype(WIDE)[0:1]
    scaled_ref[height:, :] = jnp.zeros((height, 2 * LANES), NARROW)

    row = lax.broadcasted_iota(jnp.int32, (LANES, LANES), 0)
    lane = lax.broadcasted_iota(jnp.int32, (LANES, LANES), 1)

    rolled_ref[0] = jnp.zeros((LANES, LANES), NARROW)
    before = jnp.zeros((LANES, LANES), WIDE)
    for block in range(count):
        now = jnp.broadcast_to(taps_ref[block : block + 1, :], (LANES, LANES))
        now = pltpu.roll(now, 0, 1, stride=1, stride_axis=0)
        rolled_ref[block + 1] = jnp.where(lane >= row, now, before).astype(NARROW)
        before = now

    flip = jnp.where(lane + row == LANES - 1, 1.0, 0.0).astype(NARROW)
    for half in range(2):
        turned_ref[half * LANES : (half + 1) * LANES, :] = lax.dot_general(
            flip,
            gated_ref[:, half * LANES : (half + 1) * LANES],
            (((1,), (1,)), ((), ())),
            preferred_element_type=WIDE,
        ).astype(NARROW)

    def finish(block, now, later):
        kept = jnp.where(lane <= row, now, later)
        lag_ref[block : block + 1, :] = jnp.sum(kept, axis=0, keepdims=True)

    pending = None
    odd = None
    for step in range(pairs):
        weights = jnp.concatenate(
            [
                jnp.concatenate([rolled_ref[2 * step + 1], rolled_ref[2 * step + 2]], axis=1),
                jnp.concatenate([rolled_ref[2 * step], rolled_ref[2 * step + 1]], axis=1),
            ],
            axis=0,
        )
        offset = step * CHANNELS
        conv = jnp.dot(gated_ref[: height - offset, :], weights, preferred_element_type=WIDE)
        corr = lax.dot_general(
            scaled_ref[offset:height, :], weights, (((1,), (1,)), ((), ())), preferred_element_type=WIDE
        )
        if step == 0:
            conv_ref[...] = conv
            corr_ref[...] = corr
        else:
            conv_ref[offset:, :] += conv
            corr_ref[: height - offset, :] += corr
        depth = min(height, -(-(height - offset) // 256) * 256)
        product = jnp.dot(
            turned_ref[:, :depth], scaled_ref[offset : offset + depth, :], preferred_element_type=WIDE
        )
        even = product[:LANES, :LANES] + product[LANES:, LANES:]
        even = pltpu.roll(even, 1, 1, stride=1, stride_axis=0)
        if step > 0:
            odd = odd + product[LANES:, :LANES]
            odd = pltpu.roll(odd, 1, 1, stride=1, stride_axis=0)
            finish(2 * step - 2, pending, odd)
            finish(2 * step - 1, odd, even)
        pending = even
        odd = product[:LANES, LANES:]
    odd = pltpu.roll(odd, 1, 1, stride=1, stride_axis=0)
    finish(count - 2, pending, odd)
    finish(count - 1, odd, jnp.zeros_like(odd))

    index = lax.axis_index("ctx")
    per_row = LANES // CHANNELS
    skip = skip_ref[pl.ds(index // per_row, 1), :]
    skip = pltpu.roll(jnp.broadcast_to(skip, (LANES, LANES)), LANES - index % per_row * CHANNELS, 1)
    skip = skip.T[:CHANNELS]
    skip = jnp.concatenate([skip, skip], axis=1)

    bias = jnp.zeros((CHANNELS, 2 * LANES), WIDE)
    for pair in range(pairs):
        rows = slice(pair * CHANNELS, (pair + 1) * CHANNELS)
        gated = gated_ref[rows, :].astype(WIDE)
        scaled = scaled_ref[rows, :].astype(WIDE)
        bias = bias + gated * scaled
        conv = (conv_ref[rows, :] + skip * gated).astype(NARROW)
        corr = (corr_ref[rows, :] + skip * scaled).astype(NARROW)
        for half in range(2):
            columns = slice(half * LANES, (half + 1) * LANES)
            out_ref[2 * pair + half, 0:CHANNELS, :] = conv[:, columns]
            out_ref[2 * pair + half, CHANNELS:EXTRA, :] = corr[:, columns]
    bias = jnp.broadcast_to(jnp.sum(bias, axis=1, keepdims=True), (CHANNELS, LANES))
    bias = jnp.concatenate([bias] * per_row, axis=0).T[0:1]
    bias_high = bias.astype(NARROW).astype(WIDE)
    bias_low = bias - bias_high
    place = lax.broadcasted_iota(jnp.int32, (8, LANES), 0)
    tail = jnp.where(place == 2, bias_high, jnp.where(place == 3, bias_low, 0.0))
    for block in range(count):
        lag = lag_ref[block : block + 1, :]
        lag_high = lag.astype(NARROW).astype(WIDE)
        tile = jnp.where(place == 0, lag_high, jnp.where(place == 1, lag - lag_high, tail))
        out_ref[block, EXTRA:ROWS, :] = tile.astype(NARROW)


def finish_kernel(in_ref, key_ref, value_ref, grad_ref, query_out, key_out, value_out, filter_out, bias_out):
    per_block = LANES // CHANNELS
    lane = lax.broadcasted_iota(jnp.int32, (1, LANES), 1) // CHANNELS
    for block in range(in_ref.shape[0] // per_block):
        columns = slice(block * LANES, (block + 1) * LANES)
        members = range(block * per_block, (block + 1) * per_block)
        conv = jnp.concatenate([in_ref[member, 0:CHANNELS, :] for member in members], axis=0).T.astype(WIDE)
        corr = jnp.concatenate([in_ref[member, CHANNELS:EXTRA, :] for member in members], axis=0).T.astype(WIDE)
        query_out[:, columns] = (grad_ref[:, columns].astype(WIDE) * conv).astype(NARROW)
        key_out[:, columns] = (corr * value_ref[:, columns].astype(WIDE)).astype(NARROW)
        value_out[:, columns] = (corr * key_ref[:, columns].astype(WIDE)).astype(NARROW)
        total = jnp.zeros((1, LANES), WIDE)
        for member in members:
            tile = in_ref[member, EXTRA:ROWS, :].astype(WIDE)
            filter_out[member : member + 1, :] = tile[0:1] + tile[1:2]
            total = total + jnp.where(lane == member % per_block, tile[2:3] + tile[3:4], 0.0)
        bias_out[block : block + 1, :] = total


def on_device(query_gate, key_gate, value_branch, grad_out, filters, skip_bias):
    tokens, channels = query_gate.shape
    count = lax.axis_size("ctx")
    height = count // 2 * CHANNELS
    message = jax.ShapeDtypeStruct((count, ROWS, LANES), NARROW)
    sent = pl.pallas_call(gate_kernel, out_shape=message, name="gate")(
        query_gate, key_gate, value_branch, grad_out, filters
    )
    moved = lax.all_to_all(sent, "ctx", split_axis=0, concat_axis=0, tiled=True)
    results = pl.pallas_call(
        sequence_kernel,
        out_shape=message,
        scratch_shapes=[
            pltpu.VMEM((height, 2 * LANES), NARROW),
            pltpu.VMEM((2 * height, 2 * LANES), NARROW),
            pltpu.VMEM((count, LANES), WIDE),
            pltpu.VMEM((count + 1, LANES, LANES), NARROW),
            pltpu.VMEM((2 * LANES, height), NARROW),
            pltpu.VMEM((height, 2 * LANES), WIDE),
            pltpu.VMEM((height, 2 * LANES), WIDE),
            pltpu.VMEM((count, LANES), WIDE),
        ],
        compiler_params=pltpu.CompilerParams(vmem_limit_bytes=48 * 1024 * 1024),
        name="sequence",
    )(skip_bias.reshape(channels // LANES, LANES), moved)
    back = lax.all_to_all(results, "ctx", split_axis=0, concat_axis=0, tiled=True)
    wide_out = jax.ShapeDtypeStruct((tokens, channels), NARROW)
    grad_query, grad_key, grad_value, grad_filters, grad_bias = pl.pallas_call(
        finish_kernel,
        out_shape=(
            wide_out,
            wide_out,
            wide_out,
            jax.ShapeDtypeStruct(filters.shape, WIDE),
            jax.ShapeDtypeStruct((channels // LANES, LANES), WIDE),
        ),
        name="finish",
    )(back, key_gate, value_branch, grad_out)
    return grad_query, grad_key, grad_value, grad_filters, grad_bias.reshape(channels)


def solution(mesh):
    in_specs = (
        P("ctx", "ch"),
        P("ctx", "ch"),
        P("ctx", "ch"),
        P("ctx", "ch"),
        P("ch", "ctx"),
        P("ch"),
    )
    out_specs = (P("ctx", "ch"), P("ctx", "ch"), P("ctx", "ch"), P("ch", "ctx"), P("ch"))
    return jax.shard_map(
        on_device, mesh=mesh, in_specs=in_specs, out_specs=out_specs, check_vma=False
    )
```

time: 342 us -> 111 us (0.32)
  the two profiles are of different devices: /device:TPU:2 before, /device:TPU:4 now
where the time goes in v1:
time: 111 us
  blocking collectives  101 us (91%)
  Pallas kernels  9.53 us (9%)
    all_to_all x1, blocking collectives, on_device(): moved = lax.all_to_all(sent, 'ctx', split_axis=0, concat_axis=0, tiled=True)  57.3 us
    all_to_all x1, blocking collectives, on_device(): lax.all_to_all(results, 'ctx', split_axis=0, concat_axis=0, tiled=True)  43.7 us
    pallas_call x1, Pallas kernels, on_device(): pl.pallas_call(sequence_kernel, out_shape=message, scratch_shapes=[pltpu....  4.78 us
    pallas_call x1, Pallas kernels, on_device(): pl.pallas_call(finish_kernel, out_shape=(wide_out, wide_out, wide_out, ja...  2.48 us
    pallas_call x1, Pallas kernels, on_device(): pl.pallas_call(gate_kernel, out_shape=message, name='gate')  2.27 us

profile of v1, /device:TPU:4, one launch (start us, length us, event | category | flops | bytes accessed | tf_op | source)
XLA Modules:
  0.0 111.1 jit_solution(916318843274311123)
XLA Ops:
  0.6 2.3 %gate.1 = bf16[64,40,128]{2,1,0:T(8,128)(2,1)} custom-call(bf16[128,1024]{1,0:T(8,128)(2,1)} %query_ref.1, bf16[128,1024]{1,0:T(8,128)(2,1)} %key_ref.3, bf16[128,1024]{1,0:T(8,128)(2,1)} %value_ref.3, bf16[128,1024]{1,0:T(8,128)(2,1)} %grad_ref.3, f32[64,128]{1,0:T(8,128)} %filter_ref.1), custom_call_target="tpu_custom_call" | custom-call | tf_op jit(solution)/shard_map/gate/pallas_call | solution.py:165
  2.9 0.0 copy-start
  2.9 57.3 %all_to_all.10.in_ref = bf16[64,40,128]{2,1,0:T(8,128)(2,1)S(1)} all-to-all(bf16[64,40,128]{2,1,0:T(8,128)(2,1)} %gate.1), channel_id=1, replica_groups=mesh['ctx'=64,'ch'=8] {'ctx'}, dimensions={0} | all-to-all | bytes 1310720 | tf_op jit(solution)/shard_map/all_to_all | solution.py:168
  60.2 0.0 copy-done
  60.2 4.8 %sequence.1 = bf16[64,40,128]{2,1,0:T(8,128)(2,1)S(1)} custom-call(f32[8,128]{1,0:T(8,128)S(1)} %bitcast.2, bf16[64,40,128]{2,1,0:T(8,128)(2,1)S(1)} %all_to_all.10.in_ref), custom_call_target="tpu_custom_call" | custom-call | tf_op jit(solution)/shard_map/sequence/pallas_call | solution.py:169
  65.0 43.7 %all_to_all.11.in_ref = bf16[64,40,128]{2,1,0:T(8,128)(2,1)} all-to-all(bf16[64,40,128]{2,1,0:T(8,128)(2,1)S(1)} %sequence.1), channel_id=1, replica_groups=mesh['ctx'=64,'ch'=8] {'ctx'}, dimensions={0} | all-to-all | bytes 1310720 | tf_op jit(solution)/shard_map/all_to_all | solution.py:185
  108.7 2.5 %finish.1 = (bf16[128,1024]{1,0:T(8,128)(2,1)}, bf16[128,1024]{1,0:T(8,128)(2,1)}, bf16[128,1024]{1,0:T(8,128)(2,1)}, f32[64,128]{1,0:T(8,128)}, f32[8,128]{1,0:T(8,128)}) custom-call(bf16[64,40,128]{2,1,0:T(8,128)(2,1)} %all_to_all.11.in_ref, bf16[128,1024]{1,0:T(8,128)(2,1)} %key_ref.3, bf16[128,1024]{1,0:T(8,128)(2,1)} %value_ref.3, ...), custom_call_target="tpu_custom_call" | custom-call | tf_op jit(solution)/shard_map/finish/pallas_call | solution.py:187
Async XLA Ops:
  2.9 57.3 %copy-start = (f32[1024]{0:T(1024)S(1)}, f32[1024]{0:T(1024)}, u32[]{:S(2)}) copy-start(f32[1024]{0:T(1024)} %param.11) | copy-start | bytes 12292

commit v2 on v1

--- a/solution.py
+++ b/solution.py
@@ -7,41 +7,67 @@
 
 CHANNELS = 16
 EXTRA = 2 * CHANNELS
-ROWS = EXTRA + 8
+ROWS = EXTRA + 2
 LANES = 128
+PIECE = 2 * LANES
 WIDE = jnp.float32
 NARROW = jnp.bfloat16
 
 
-def gate_kernel(query_ref, key_ref, value_ref, grad_ref, filter_ref, out_ref):
-    blocks = query_ref.shape[1] // LANES
+def gate_kernel(
+    query_ref, key_ref, value_ref, grad_ref, filter_ref, out_ref, held_ref, taps_ref, sems, taps_sem
+):
     per_block = LANES // CHANNELS
-    for block in range(blocks):
-        columns = slice(block * LANES, (block + 1) * LANES)
-        gated = (key_ref[:, columns].astype(WIDE) * value_ref[:, columns].astype(WIDE)).astype(NARROW)
-        scaled = (query_ref[:, columns].astype(WIDE) * grad_ref[:, columns].astype(WIDE)).astype(NARROW)
-        gated, scaled = gated.T, scaled.T
-        for part in range(per_block):
-            rows = slice(part * CHANNELS, (part + 1) * CHANNELS)
-            out_ref[block * per_block + part, 0:CHANNELS, :] = gated[rows]
-            out_ref[block * per_block + part, CHANNELS:EXTRA, :] = scaled[rows]
+    pieces = query_ref.shape[1] // PIECE
+    copies = []
+    for piece in range(pieces):
+        columns = pl.ds(piece * PIECE, PIECE)
+        copies.append(
+            [
+                pltpu.make_async_copy(
+                    source.at[:, columns], held_ref.at[place, :, columns], sems.at[piece, place]
+                )
+                for place, source in enumerate((key_ref, value_ref, query_ref, grad_ref))
+            ]
+        )
+    taps_copy = pltpu.make_async_copy(filter_ref, taps_ref, taps_sem)
+    for group in copies:
+        for copy in group:
+            copy.start()
+    taps_copy.start()
+
+    for piece in range(pieces):
+        for copy in copies[piece]:
+            copy.wait()
+        for block in range(piece * PIECE // LANES, (piece + 1) * PIECE // LANES):
+            columns = slice(block * LANES, (block + 1) * LANES)
+            key, value, query, grad = (held_ref[place, :, columns].astype(WIDE) for place in range(4))
+            gated = (key * value).astype(NARROW).T
+            scaled = (query * grad).astype(NARROW).T
+            for part in range(per_block):
+                rows = slice(part * CHANNELS, (part + 1) * CHANNELS)
+                first = (block * per_block + part) * ROWS
+                out_ref[first : first + CHANNELS, :] = gated[rows]
+                out_ref[first + CHANNELS : first + EXTRA, :] = scaled[rows]
+    taps_copy.wait()
     for group in range(filter_ref.shape[0]):
-        taps = jnp.broadcast_to(filter_ref[group : group + 1, :], (8, LANES))
-        out_ref[group, EXTRA:ROWS, :] = taps.astype(NARROW)
+        taps = jnp.broadcast_to(taps_ref[group : group + 1, :], (2, LANES))
+        out_ref[group * ROWS + EXTRA : (group + 1) * ROWS, :] = taps.astype(NARROW)
 
 
 def sequence_kernel(
     skip_ref, in_ref, out_ref, gated_ref, scaled_ref, taps_ref, rolled_ref, turned_ref, conv_ref, corr_ref, lag_ref
 ):
-    count = in_ref.shape[0]
+    count = in_ref.shape[0] // ROWS
     pairs = count // 2
     height = pairs * CHANNELS
     for block in range(count):
         rows = slice(block // 2 * CHANNELS, (block // 2 + 1) * CHANNELS)
         columns = slice(block % 2 * LANES, (block % 2 + 1) * LANES)
-        gated_ref[rows, columns] = in_ref[block, 0:CHANNELS, :]
-        scaled_ref[rows, columns] = in_ref[block, CHANNELS:EXTRA, :]
-        taps_ref[block : block + 1, :] = in_ref[block, EXTRA:ROWS, :].astype(WIDE)[0:1]
+        first = block * ROWS
+        gated_ref[rows, columns] = in_ref[first : first + CHANNELS, :]
+        scaled_ref[rows, columns] = in_ref[first + CHANNELS : first + EXTRA, :]
+        taps_ref[block : block + 1, :] = in_ref[first + EXTRA : first + ROWS, :].astype(WIDE)[0:1]
     scaled_ref[height:, :] = jnp.zeros((height, 2 * LANES), NARROW)
 
     row = lax.broadcasted_iota(jnp.int32, (LANES, LANES), 0)
@@ -123,49 +149,94 @@
         corr = (corr_ref[rows, :] + skip * scaled).astype(NARROW)
         for half in range(2):
             columns = slice(half * LANES, (half + 1) * LANES)
-            out_ref[2 * pair + half, 0:CHANNELS, :] = conv[:, columns]
-            out_ref[2 * pair + half, CHANNELS:EXTRA, :] = corr[:, columns]
+            first = (2 * pair + half) * ROWS
+            out_ref[first : first + CHANNELS, :] = conv[:, columns]
+            out_ref[first + CHANNELS : first + EXTRA, :] = corr[:, columns]
     bias = jnp.broadcast_to(jnp.sum(bias, axis=1, keepdims=True), (CHANNELS, LANES))
     bias = jnp.concatenate([bias] * per_row, axis=0).T[0:1]
     bias_high = bias.astype(NARROW).astype(WIDE)
-    bias_low = bias - bias_high
-    place = lax.broadcasted_iota(jnp.int32, (8, LANES), 0)
-    tail = jnp.where(place == 2, bias_high, jnp.where(place == 3, bias_low, 0.0))
+    even = lax.broadcasted_iota(jnp.int32, (1, LANES), 1) // CHANNELS % 2 == 0
+    tail = jnp.where(even, bias_high, bias - bias_high)
     for block in range(count):
-        lag = lag_ref[block : block + 1, :]
-        lag_high = lag.astype(NARROW).astype(WIDE)
-        tile = jnp.where(place == 0, lag_high, jnp.where(place == 1, lag - lag_high, tail))
-        out_ref[block, EXTRA:ROWS, :] = tile.astype(NARROW)
-
-
-def finish_kernel(in_ref, key_ref, value_ref, grad_ref, query_out, key_out, value_out, filter_out, bias_out):
+        rows = jnp.concatenate([lag_ref[block : block + 1, :], tail], axis=0)
+        out_ref[block * ROWS + EXTRA : (block + 1) * ROWS, :] = rows.astype(NARROW)
+
+
+def finish_kernel(
+    in_ref, key_ref, value_ref, grad_ref, query_out, key_out, value_out, filter_out, bias_out, held_ref, sems
+):
     per_block = LANES // CHANNELS
     lane = lax.broadcasted_iota(jnp.int32, (1, LANES), 1) // CHANNELS
-    for block in range(in_ref.shape[0] // per_block):
-        columns = slice(block * LANES, (block + 1) * LANES)
-        members = range(block * per_block, (block + 1) * per_block)
-        conv = jnp.concatenate([in_ref[member, 0:CHANNELS, :] for member in members], axis=0).T.astype(WIDE)
-        corr = jnp.concatenate([in_ref[member, CHANNELS:EXTRA, :] for member in members], axis=0).T.astype(WIDE)
-        query_out[:, columns] = (grad_ref[:, columns].astype(WIDE) * conv).astype(NARROW)
-        key_out[:, columns] = (corr * value_ref[:, columns].astype(WIDE)).astype(NARROW)
-        value_out[:, columns] = (corr * key_ref[:, columns].astype(WIDE)).astype(NARROW)
+    copies = []
+    for piece in range(key_ref.shape[1] // PIECE):
+        for block in range(piece * PIECE // LANES, (piece + 1) * PIECE // LANES):
+            columns = slice(block * LANES, (block + 1) * LANES)
+            members = range(block * per_block, (block + 1) * per_block)
+
+            def gather(offset):
+                parts = [in_ref[member * ROWS + offset : member * ROWS + offset + CHANNELS, :] for member in members]
+                return jnp.concatenate(parts, axis=0).T.astype(WIDE)
+
+            conv, corr = gather(0), gather(CHANNELS)
+            held_ref[0, :, columns] = (grad_ref[:, columns].astype(WIDE) * conv).astype(NARROW)
+            held_ref[1, :, columns] = (corr * value_ref[:, columns].astype(WIDE)).astype(NARROW)
+            held_ref[2, :, columns] = (corr * key_ref[:, columns].astype(WIDE)).astype(NARROW)
+        columns = pl.ds(piece * PIECE, PIECE)
+        for place, target in enumerate((query_out, key_out, value_out)):
+            copy = pltpu.make_async_copy(
+                held_ref.at[place, :, columns], target.at[:, columns], sems.at[piece, place]
+            )
+            copy.start()
+            copies.append(copy)
+
+    for block in range(key_ref.shape[1] // LANES):
         total = jnp.zeros((1, LANES), WIDE)
-        for member in members:
-            tile = in_ref[member, EXTRA:ROWS, :].astype(WIDE)
-            filter_out[member : member + 1, :] = tile[0:1] + tile[1:2]
-            total = total + jnp.where(lane == member % per_block, tile[2:3] + tile[3:4], 0.0)
+        for part in range(per_block):
+            member = block * per_block + part
+            rows = in_ref[member * ROWS + EXTRA : (member + 1) * ROWS, :].astype(WIDE)
+            filter_out[member : member + 1, :] = rows[0:1]
+            both = rows[1:2] + pltpu.roll(rows[1:2], CHANNELS, 1)
+            total = total + jnp.where(lane == part, both, 0.0)
         bias_out[block : block + 1, :] = total
+    for copy in copies:
+        copy.wait()
+
+
+def exchange(messages):
+    count = lax.axis_size("ctx")
+    split = messages.reshape(count, ROWS // 2, 2, LANES)
+    return lax.all_to_all(split, "ctx", split_axis=0, concat_axis=0, tiled=True).reshape(messages.shape)
 
 
 def on_device(query_gate, key_gate, value_branch, grad_out, filters, skip_bias):
     tokens, channels = query_gate.shape
     count = lax.axis_size("ctx")
     height = count // 2 * CHANNELS
-    message = jax.ShapeDtypeStruct((count, ROWS, LANES), NARROW)
-    sent = pl.pallas_call(gate_kernel, out_shape=message, name="gate")(
-        query_gate, key_gate, value_branch, grad_out, filters
+    message = jax.ShapeDtypeStruct((count * ROWS, LANES), NARROW)
+    grant = pltpu.CompilerParams(vmem_limit_bytes=16 * 1024 * 1024)
+    hbm = pl.BlockSpec(memory_space=pltpu.HBM)
+    vmem = pl.BlockSpec(memory_space=pltpu.VMEM)
+    pieces = channels // PIECE
+    sent = pl.pallas_call(
+        gate_kernel,
+        out_shape=message,
+        in_specs=[hbm] * 5,
+        out_specs=vmem,
+        scratch_shapes=[
+            pltpu.VMEM((4, tokens, channels), NARROW),
+            pltpu.VMEM(filters.shape, WIDE),
+            pltpu.SemaphoreType.DMA((pieces, 4)),
+            pltpu.SemaphoreType.DMA,
+        ],
+        compiler_params=grant,
+        name="gate",
+    )(
+        *(
+            pltpu.with_memory_space_constraint(argument, pltpu.HBM)
+            for argument in (query_gate, key_gate, value_branch, grad_out, filters)
+        )
     )
-    moved = lax.all_to_all(sent, "ctx", split_axis=0, concat_axis=0, tiled=True)
+    moved = exchange(sent)
     results = pl.pallas_call(
         sequence_kernel,
         out_shape=message,
@@ -179,10 +250,10 @@
             pltpu.VMEM((height, 2 * LANES), WIDE),
             pltpu.VMEM((count, LANES), WIDE),
         ],
-        compiler_params=pltpu.CompilerParams(vmem_limit_bytes=48 * 1024 * 1024),
+        compiler_params=grant,
         name="sequence",
     )(skip_bias.reshape(channels // LANES, LANES), moved)
-    back = lax.all_to_all(results, "ctx", split_axis=0, concat_axis=0, tiled=True)
+    back = exchange(results)
     wide_out = jax.ShapeDtypeStruct((tokens, channels), NARROW)
     grad_query, grad_key, grad_value, grad_filters, grad_bias = pl.pallas_call(
         finish_kernel,
@@ -193,6 +264,13 @@
             jax.ShapeDtypeStruct(filters.shape, WIDE),
             jax.ShapeDtypeStruct((channels // LANES, LANES), WIDE),
         ),
+        in_specs=[vmem] * 4,
+        out_specs=(hbm, hbm, hbm, vmem, vmem),
+        scratch_shapes=[
+            pltpu.VMEM((3, tokens, channels), NARROW),
+            pltpu.SemaphoreType.DMA((pieces, 3)),
+        ],
+        compiler_params=grant,
         name="finish",
     )(back, key_gate, value_branch, grad_out)
     return grad_query, grad_key, grad_value, grad_filters, grad_bias.reshape(channels)

time: 111 us -> 101 us (0.910)
  the two profiles are of different devices: /device:TPU:4 before, /device:TPU:2 now
where the time goes in v2:
time: 101 us
  blocking collectives  91.9 us (91%)
  Pallas kernels  8.3 us (8%)
    all_to_all x2, blocking collectives, exchange(): lax.all_to_all(split, 'ctx', split_axis=0, concat_axis=0, tiled=True)  91.9 us
    pallas_call x1, Pallas kernels, on_device(): pl.pallas_call(sequence_kernel, out_shape=message, scratch_shapes=[pltpu....  4.97 us

profile of v2, /device:TPU:2, one launch (start us, length us, event | category | flops | bytes accessed | tf_op | source)
XLA Modules:
  0.0 100.9 jit_solution(16214065559368864766)
XLA Ops:
  0.6 1.6 %gate.1 = bf16[2176,128]{1,0:T(8,128)(2,1)S(1)} custom-call(bf16[128,1024]{1,0:T(8,128)(2,1)} %query_ref.1, bf16[128,1024]{1,0:T(8,128)(2,1)} %key_ref.3, bf16[128,1024]{1,0:T(8,128)(2,1)} %value_ref.3, bf16[128,1024]{1,0:T(8,128)(2,1)} %grad_ref.3, f32[64,128]{1,0:T(8,128)} %filter_ref.1), custom_call_target="tpu_custom_call" | custom-call | tf_op jit(solution)/shard_map/gate/pallas_call | solution.py:220
  2.2 0.0 copy-start.3
  2.2 52.8 %all_to_all.10 = bf16[64,17,2,128]{3,2,1,0:T(2,128)(2,1)S(1)} all-to-all(bf16[64,17,2,128]{3,2,1,0:T(2,128)(2,1)S(1)} %bitcast.9), channel_id=1, replica_groups=mesh['ctx'=64,'ch'=8] {'ctx'}, dimensions={0} | all-to-all | bytes 1114112 | tf_op jit(solution)/shard_map/all_to_all | solution.py:208
  55.0 0.0 copy-done.3
  55.0 5.0 %sequence.1 = bf16[2176,128]{1,0:T(8,128)(2,1)S(1)} custom-call(f32[8,128]{1,0:T(8,128)S(1)} %bitcast.10, bf16[2176,128]{1,0:T(8,128)(2,1)S(1)} %bitcast.7), custom_call_target="tpu_custom_call" | custom-call | tf_op jit(solution)/shard_map/sequence/pallas_call | solution.py:240
  60.0 0.0 copy-start
  60.0 0.0 copy-start.1
  60.0 0.0 copy-start.2
  60.0 39.2 %all_to_all.11 = bf16[64,17,2,128]{3,2,1,0:T(2,128)(2,1)S(1)} all-to-all(bf16[64,17,2,128]{3,2,1,0:T(2,128)(2,1)S(1)} %bitcast.8), channel_id=1, replica_groups=mesh['ctx'=64,'ch'=8] {'ctx'}, dimensions={0} | all-to-all | bytes 1114112 | tf_op jit(solution)/shard_map/all_to_all | solution.py:208
  99.2 0.0 copy-done
  99.2 0.0 copy-done.1
  99.2 0.0 copy-done.2
  99.2 1.7 %finish.1 = (bf16[128,1024]{1,0:T(8,128)(2,1)}, bf16[128,1024]{1,0:T(8,128)(2,1)}, bf16[128,1024]{1,0:T(8,128)(2,1)}, f32[64,128]{1,0:T(8,128)}, f32[8,128]{1,0:T(8,128)}) custom-call(bf16[2176,128]{1,0:T(8,128)(2,1)S(1)} %bitcast.6, bf16[128,1024]{1,0:T(8,128)(2,1)S(1)} %copy-done, bf16[128,1024]{1,0:T(8,128)(2,1)S(1)} %copy-done.1, ...), custom_call_target="tpu_custom_call" | custom-call | tf_op jit(solution)/shard_map/finish/pallas_call | solution.py:258
Async XLA Ops:
  2.2 52.8 %copy-start.3 = (f32[1024]{0:T(1024)S(1)}, f32[1024]{0:T(1024)}, u32[]{:S(2)}) copy-start(f32[1024]{0:T(1024)} %param.11) | copy-start | bytes 12292
  60.0 39.2 %copy-start = (bf16[128,1024]{1,0:T(8,128)(2,1)S(1)}, bf16[128,1024]{1,0:T(8,128)(2,1)}, u32[]{:S(2)}) copy-start(bf16[128,1024]{1,0:T(8,128)(2,1)} %key_ref.3) | copy-start | bytes 786436
  60.0 39.2 %copy-start.1 = (bf16[128,1024]{1,0:T(8,128)(2,1)S(1)}, bf16[128,1024]{1,0:T(8,128)(2,1)}, u32[]{:S(2)}) copy-start(bf16[128,1024]{1,0:T(8,128)(2,1)} %value_ref.3) | copy-start | bytes 786436
  60.0 39.2 %copy-start.2 = (bf16[128,1024]{1,0:T(8,128)(2,1)S(1)}, bf16[128,1024]{1,0:T(8,128)(2,1)}, u32[]{:S(2)}) copy-start(bf16[128,1024]{1,0:T(8,128)(2,1)} %grad_ref.3) | copy-start | bytes 786436

commit v3 on v2

--- a/solution.py
+++ b/solution.py
@@ -10,8 +10,20 @@
 ROWS = EXTRA + 2
 LANES = 128
 PIECE = 2 * LANES
+SIDE = 4
+STEP = 9
 WIDE = jnp.float32
 NARROW = jnp.bfloat16
+
+
+def listing(count):
+    ring = count // SIDE
+    return [STEP * turn % ring * SIDE + place for place in range(SIDE) for turn in range(ring)]
+
+
+def first_rows(count):
+    order = listing(count)
+    return [order.index(device) * ROWS for device in range(count)]
 
 
 def gate_kernel(
@@ -19,6 +31,7 @@
 ):
     per_block = LANES // CHANNELS
     pieces = query_ref.shape[1] // PIECE
+    starts = first_rows(filter_ref.shape[0])
     copies = []
     for piece in range(pieces):
         columns = pl.ds(piece * PIECE, PIECE)
@@ -46,25 +59,26 @@
             scaled = (query * grad).astype(NARROW).T
             for part in range(per_block):
                 rows = slice(part * CHANNELS, (part + 1) * CHANNELS)
-                first = (block * per_block + part) * ROWS
+                first = starts[block * per_block + part]
                 out_ref[first : first + CHANNELS, :] = gated[rows]
                 out_ref[first + CHANNELS : first + EXTRA, :] = scaled[rows]
     taps_copy.wait()
     for group in range(filter_ref.shape[0]):
         taps = jnp.broadcast_to(taps_ref[group : group + 1, :], (2, LANES))
-        out_ref[group * ROWS + EXTRA : (group + 1) * ROWS, :] = taps.astype(NARROW)
+        out_ref[starts[group] + EXTRA : starts[group] + ROWS, :] = taps.astype(NARROW)
 
 
 def sequence_kernel(
     skip_ref, in_ref, out_ref, gated_ref, scaled_ref, taps_ref, rolled_ref, turned_ref, conv_ref, corr_ref, lag_ref
 ):
     count = in_ref.shape[0] // ROWS
+    starts = first_rows(count)
     pairs = count // 2
     height = pairs * CHANNELS
     for block in range(count):
         rows = slice(block // 2 * CHANNELS, (block // 2 + 1) * CHANNELS)
         columns = slice(block % 2 * LANES, (block % 2 + 1) * LANES)
-        first = block * ROWS
+        first = starts[block]
         gated_ref[rows, columns] = in_ref[first : first + CHANNELS, :]
         scaled_ref[rows, columns] = in_ref[first + CHANNELS : first + EXTRA, :]
         taps_ref[block : block + 1, :] = in_ref[first + EXTRA : first + ROWS, :].astype(WIDE)[0:1]
@@ -149,7 +163,7 @@
         corr = (corr_ref[rows, :] + skip * scaled).astype(NARROW)
         for half in range(2):
             columns = slice(half * LANES, (half + 1) * LANES)
-            first = (2 * pair + half) * ROWS
+            first = starts[2 * pair + half]
             out_ref[first : first + CHANNELS, :] = conv[:, columns]
             out_ref[first + CHANNELS : first + EXTRA, :] = corr[:, columns]
     bias = jnp.broadcast_to(jnp.sum(bias, axis=1, keepdims=True), (CHANNELS, LANES))
@@ -159,7 +173,7 @@
     tail = jnp.where(even, bias_high, bias - bias_high)
     for block in range(count):
         rows = jnp.concatenate([lag_ref[block : block + 1, :], tail], axis=0)
-        out_ref[block * ROWS + EXTRA : (block + 1) * ROWS, :] = rows.astype(NARROW)
+        out_ref[starts[block] + EXTRA : starts[block] + ROWS, :] = rows.astype(NARROW)
 
 
 def finish_kernel(
@@ -167,6 +181,7 @@
 ):
     per_block = LANES // CHANNELS
     lane = lax.broadcasted_iota(jnp.int32, (1, LANES), 1) // CHANNELS
+    starts = first_rows(filter_out.shape[0])
     copies = []
     for piece in range(key_ref.shape[1] // PIECE):
         for block in range(piece * PIECE // LANES, (piece + 1) * PIECE // LANES):
@@ -174,7 +189,7 @@
             members = range(block * per_block, (block + 1) * per_block)
 
             def gather(offset):
-                parts = [in_ref[member * ROWS + offset : member * ROWS + offset + CHANNELS, :] for member in members]
+                parts = [in_ref[starts[member] + offset : starts[member] + offset + CHANNELS, :] for member in members]
                 return jnp.concatenate(parts, axis=0).T.astype(WIDE)
 
             conv, corr = gather(0), gather(CHANNELS)
@@ -193,7 +208,7 @@
         total = jnp.zeros((1, LANES), WIDE)
         for part in range(per_block):
             member = block * per_block + part
-            rows = in_ref[member * ROWS + EXTRA : (member + 1) * ROWS, :].astype(WIDE)
+            rows = in_ref[starts[member] + EXTRA : starts[member] + ROWS, :].astype(WIDE)
             filter_out[member : member + 1, :] = rows[0:1]
             both = rows[1:2] + pltpu.roll(rows[1:2], CHANNELS, 1)
             total = total + jnp.where(lane == part, both, 0.0)
@@ -205,7 +220,10 @@
 def exchange(messages):
     count = lax.axis_size("ctx")
     split = messages.reshape(count, ROWS // 2, 2, LANES)
-    return lax.all_to_all(split, "ctx", split_axis=0, concat_axis=0, tiled=True).reshape(messages.shape)
+    moved = lax.all_to_all(
+        split, "ctx", split_axis=0, concat_axis=0, tiled=True, axis_index_groups=[listing(count)]
+    )
+    return moved.reshape(messages.shape)
 
 
 def on_device(query_gate, key_gate, value_branch, grad_out, filters, skip_bias):

time: 101 us -> 99.7 us (0.987)
  the two profiles are of different devices: /device:TPU:2 before, /device:TPU:36 now
where the time goes in v3:
time: 99.7 us; the launch traced here: 99.4 us
  blocking collectives  90.4 us (91%)
  Pallas kernels  8.3 us (8%)
    all_to_all x2, blocking collectives, exchange(): lax.all_to_all(split, 'ctx', split_axis=0, concat_axis=0, tiled=True, axi...  90.4 us
    pallas_call x1, Pallas kernels, on_device(): pl.pallas_call(sequence_kernel, out_shape=message, scratch_shapes=[pltpu....  4.97 us

profile of v3, /device:TPU:36, one launch (start us, length us, event | category | flops | bytes accessed | tf_op | source)
XLA Modules:
  0.0 99.4 jit_solution(2952492903258524942)
XLA Ops:
  0.6 1.6 %gate.1 = bf16[2176,128]{1,0:T(8,128)(2,1)S(1)} custom-call(bf16[128,1024]{1,0:T(8,128)(2,1)} %query_ref.1, bf16[128,1024]{1,0:T(8,128)(2,1)} %key_ref.3, bf16[128,1024]{1,0:T(8,128)(2,1)} %value_ref.3, bf16[128,1024]{1,0:T(8,128)(2,1)} %grad_ref.3, f32[64,128]{1,0:T(8,128)} %filter_ref.1), custom_call_target="tpu_custom_call" | custom-call | tf_op jit(solution)/shard_map/gate/pallas_call | solution.py:238
  2.2 0.0 copy-start.3
  2.2 51.4 %all_to_all.10 = bf16[64,17,2,128]{3,2,1,0:T(2,128)(2,1)S(1)} all-to-all(bf16[64,17,2,128]{3,2,1,0:T(2,128)(2,1)S(1)} %bitcast.9), channel_id=1, replica_groups={{0,288,64,352,128,416,192,480,256,32,320,96,384,160,448,224,8,296,72,36..., dimensions={0} | all-to-all | bytes 1114112 | tf_op jit(solution)/shard_map/all_to_all | solution.py:223
  53.7 0.0 copy-done.3
  53.7 5.0 %sequence.1 = bf16[2176,128]{1,0:T(8,128)(2,1)S(1)} custom-call(f32[8,128]{1,0:T(8,128)S(1)} %bitcast.10, bf16[2176,128]{1,0:T(8,128)(2,1)S(1)} %bitcast.7), custom_call_target="tpu_custom_call" | custom-call | tf_op jit(solution)/shard_map/sequence/pallas_call | solution.py:258
  58.6 0.0 copy-start
  58.7 0.0 copy-start.1
  58.7 0.0 copy-start.2
  58.7 39.0 %all_to_all.11 = bf16[64,17,2,128]{3,2,1,0:T(2,128)(2,1)S(1)} all-to-all(bf16[64,17,2,128]{3,2,1,0:T(2,128)(2,1)S(1)} %bitcast.8), channel_id=1, replica_groups={{0,288,64,352,128,416,192,480,256,32,320,96,384,160,448,224,8,296,72,36..., dimensions={0} | all-to-all | bytes 1114112 | tf_op jit(solution)/shard_map/all_to_all | solution.py:223
  97.6 0.0 copy-done
  97.7 0.0 copy-done.1
  97.7 0.0 copy-done.2
  97.7 1.7 %finish.1 = (bf16[128,1024]{1,0:T(8,128)(2,1)}, bf16[128,1024]{1,0:T(8,128)(2,1)}, bf16[128,1024]{1,0:T(8,128)(2,1)}, f32[64,128]{1,0:T(8,128)}, f32[8,128]{1,0:T(8,128)}) custom-call(bf16[2176,128]{1,0:T(8,128)(2,1)S(1)} %bitcast.6, bf16[128,1024]{1,0:T(8,128)(2,1)S(1)} %copy-done, bf16[128,1024]{1,0:T(8,128)(2,1)S(1)} %copy-done.1, ...), custom_call_target="tpu_custom_call" | custom-call | tf_op jit(solution)/shard_map/finish/pallas_call | solution.py:276
Async XLA Ops:
  2.2 51.4 %copy-start.3 = (f32[1024]{0:T(1024)S(1)}, f32[1024]{0:T(1024)}, u32[]{:S(2)}) copy-start(f32[1024]{0:T(1024)} %param.11) | copy-start | bytes 12292
  58.6 39.0 %copy-start = (bf16[128,1024]{1,0:T(8,128)(2,1)S(1)}, bf16[128,1024]{1,0:T(8,128)(2,1)}, u32[]{:S(2)}) copy-start(bf16[128,1024]{1,0:T(8,128)(2,1)} %key_ref.3) | copy-start | bytes 786436
  58.7 39.0 %copy-start.1 = (bf16[128,1024]{1,0:T(8,128)(2,1)S(1)}, bf16[128,1024]{1,0:T(8,128)(2,1)}, u32[]{:S(2)}) copy-start(bf16[128,1024]{1,0:T(8,128)(2,1)} %value_ref.3) | copy-start | bytes 786436
  58.7 39.0 %copy-start.2 = (bf16[128,1024]{1,0:T(8,128)(2,1)S(1)}, bf16[128,1024]{1,0:T(8,128)(2,1)}, u32[]{:S(2)}) copy-start(bf16[128,1024]{1,0:T(8,128)(2,1)} %grad_ref.3) | copy-start | bytes 786436

commit v4 on v3

--- a/solution.py
+++ b/solution.py
@@ -9,7 +9,7 @@
 EXTRA = 2 * CHANNELS
 ROWS = EXTRA + 2
 LANES = 128
-PIECE = 2 * LANES
+PIECE = 4 * LANES
 SIDE = 4
 STEP = 9
 WIDE = jnp.float32
@@ -54,9 +54,9 @@
             copy.wait()
         for block in range(piece * PIECE // LANES, (piece + 1) * PIECE // LANES):
             columns = slice(block * LANES, (block + 1) * LANES)
-            key, value, query, grad = (held_ref[place, :, columns].astype(WIDE) for place in range(4))
-            gated = (key * value).astype(NARROW).T
-            scaled = (query * grad).astype(NARROW).T
+            key, value, query, grad = (held_ref[place, :, columns] for place in range(4))
+            both = jnp.concatenate([key * value, query * grad], axis=1).T
+            gated, scaled = both[:LANES], both[LANES:]
             for part in range(per_block):
                 rows = slice(part * CHANNELS, (part + 1) * CHANNELS)
                 first = starts[block * per_block + part]
@@ -190,12 +190,12 @@
 
             def gather(offset):
                 parts = [in_ref[starts[member] + offset : starts[member] + offset + CHANNELS, :] for member in members]
-                return jnp.concatenate(parts, axis=0).T.astype(WIDE)
+                return jnp.concatenate(parts, axis=0).T
 
             conv, corr = gather(0), gather(CHANNELS)
-            held_ref[0, :, columns] = (grad_ref[:, columns].astype(WIDE) * conv).astype(NARROW)
-            held_ref[1, :, columns] = (corr * value_ref[:, columns].astype(WIDE)).astype(NARROW)
-            held_ref[2, :, columns] = (corr * key_ref[:, columns].astype(WIDE)).astype(NARROW)
+            held_ref[0, :, columns] = grad_ref[:, columns] * conv
+            held_ref[1, :, columns] = corr * value_ref[:, columns]
+            held_ref[2, :, columns] = corr * key_ref[:, columns]
         columns = pl.ds(piece * PIECE, PIECE)
         for place, target in enumerate((query_out, key_out, value_out)):
             copy = pltpu.make_async_copy(

time: 99.7 us -> 99.6 us (level)
  no operation moved by 1% of the time
where the time goes in v4:
time: 99.6 us; the launch traced here: 99.3 us
  blocking collectives  90.4 us (91%)
  Pallas kernels  8.25 us (8%)
    all_to_all x2, blocking collectives, exchange(): lax.all_to_all(split, 'ctx', split_axis=0, concat_axis=0, tiled=True, axi...  90.4 us
    pallas_call x1, Pallas kernels, on_device(): pl.pallas_call(sequence_kernel, out_shape=message, scratch_shapes=[pltpu....  4.97 us

profile of v4, /device:TPU:36, one launch (start us, length us, event | category | flops | bytes accessed | tf_op | source)
XLA Modules:
  0.0 99.3 jit_solution(3238786948426439806)
XLA Ops:
  0.6 1.5 %gate.1 = bf16[2176,128]{1,0:T(8,128)(2,1)S(1)} custom-call(bf16[128,1024]{1,0:T(8,128)(2,1)} %query_ref.1, bf16[128,1024]{1,0:T(8,128)(2,1)} %key_ref.3, bf16[128,1024]{1,0:T(8,128)(2,1)} %value_ref.3, bf16[128,1024]{1,0:T(8,128)(2,1)} %grad_ref.3, f32[64,128]{1,0:T(8,128)} %filter_ref.1), custom_call_target="tpu_custom_call" | custom-call | tf_op jit(solution)/shard_map/gate/pallas_call | solution.py:238
  2.2 0.0 copy-start.3
  2.2 51.4 %all_to_all.10 = bf16[64,17,2,128]{3,2,1,0:T(2,128)(2,1)S(1)} all-to-all(bf16[64,17,2,128]{3,2,1,0:T(2,128)(2,1)S(1)} %bitcast.9), channel_id=1, replica_groups={{0,288,64,352,128,416,192,480,256,32,320,96,384,160,448,224,8,296,72,36..., dimensions={0} | all-to-all | bytes 1114112 | tf_op jit(solution)/shard_map/all_to_all | solution.py:223
  53.6 0.0 copy-done.3
  53.6 5.0 %sequence.1 = bf16[2176,128]{1,0:T(8,128)(2,1)S(1)} custom-call(f32[8,128]{1,0:T(8,128)S(1)} %bitcast.10, bf16[2176,128]{1,0:T(8,128)(2,1)S(1)} %bitcast.7), custom_call_target="tpu_custom_call" | custom-call | tf_op jit(solution)/shard_map/sequence/pallas_call | solution.py:258
  58.6 0.0 copy-start
  58.6 0.0 copy-start.1
  58.6 0.0 copy-start.2
  58.6 39.0 %all_to_all.11 = bf16[64,17,2,128]{3,2,1,0:T(2,128)(2,1)S(1)} all-to-all(bf16[64,17,2,128]{3,2,1,0:T(2,128)(2,1)S(1)} %bitcast.8), channel_id=1, replica_groups={{0,288,64,352,128,416,192,480,256,32,320,96,384,160,448,224,8,296,72,36..., dimensions={0} | all-to-all | bytes 1114112 | tf_op jit(solution)/shard_map/all_to_all | solution.py:223
  97.6 0.0 copy-done
  97.6 0.0 copy-done.1
  97.6 0.0 copy-done.2
  97.6 1.7 %finish.1 = (bf16[128,1024]{1,0:T(8,128)(2,1)}, bf16[128,1024]{1,0:T(8,128)(2,1)}, bf16[128,1024]{1,0:T(8,128)(2,1)}, f32[64,128]{1,0:T(8,128)}, f32[8,128]{1,0:T(8,128)}) custom-call(bf16[2176,128]{1,0:T(8,128)(2,1)S(1)} %bitcast.6, bf16[128,1024]{1,0:T(8,128)(2,1)S(1)} %copy-done, bf16[128,1024]{1,0:T(8,128)(2,1)S(1)} %copy-done.1, ...), custom_call_target="tpu_custom_call" | custom-call | tf_op jit(solution)/shard_map/finish/pallas_call | solution.py:276
Async XLA Ops:
  2.2 51.4 %copy-start.3 = (f32[1024]{0:T(1024)S(1)}, f32[1024]{0:T(1024)}, u32[]{:S(2)}) copy-start(f32[1024]{0:T(1024)} %param.11) | copy-start | bytes 12292
  58.6 39.0 %copy-start = (bf16[128,1024]{1,0:T(8,128)(2,1)S(1)}, bf16[128,1024]{1,0:T(8,128)(2,1)}, u32[]{:S(2)}) copy-start(bf16[128,1024]{1,0:T(8,128)(2,1)} %key_ref.3) | copy-start | bytes 786436
  58.6 39.0 %copy-start.1 = (bf16[128,1024]{1,0:T(8,128)(2,1)S(1)}, bf16[128,1024]{1,0:T(8,128)(2,1)}, u32[]{:S(2)}) copy-start(bf16[128,1024]{1,0:T(8,128)(2,1)} %value_ref.3) | copy-start | bytes 786436
  58.6 39.0 %copy-start.2 = (bf16[128,1024]{1,0:T(8,128)(2,1)S(1)}, bf16[128,1024]{1,0:T(8,128)(2,1)}, u32[]{:S(2)}) copy-start(bf16[128,1024]{1,0:T(8,128)(2,1)} %grad_ref.3) | copy-start | bytes 786436

commit v5 on v3

--- a/solution.py
+++ b/solution.py
@@ -9,20 +9,22 @@
 EXTRA = 2 * CHANNELS
 ROWS = EXTRA + 2
 LANES = 128
-PIECE = 2 * LANES
+PIECE = 4 * LANES
 SIDE = 4
 STEP = 9
+STEP_BACK = 13
 WIDE = jnp.float32
 NARROW = jnp.bfloat16
 
 
-def listing(count):
+def listing(count, back=False):
     ring = count // SIDE
-    return [STEP * turn % ring * SIDE + place for place in range(SIDE) for turn in range(ring)]
-
-
-def first_rows(count):
-    order = listing(count)
+    step = STEP_BACK if back else STEP
+    return [step * turn % ring * SIDE + place for place in range(SIDE) for turn in range(ring)]
+
+
+def first_rows(count, back=False):
+    order = listing(count, back)
     return [order.index(device) * ROWS for device in range(count)]
 
 
@@ -54,9 +56,9 @@
             copy.wait()
         for block in range(piece * PIECE // LANES, (piece + 1) * PIECE // LANES):
             columns = slice(block * LANES, (block + 1) * LANES)
-            key, value, query, grad = (held_ref[place, :, columns].astype(WIDE) for place in range(4))
-            gated = (key * value).astype(NARROW).T
-            scaled = (query * grad).astype(NARROW).T
+            key, value, query, grad = (held_ref[place, :, columns] for place in range(4))
+            gated = (key * value).T
+            scaled = (query * grad).T
             for part in range(per_block):
                 rows = slice(part * CHANNELS, (part + 1) * CHANNELS)
                 first = starts[block * per_block + part]
@@ -73,6 +75,7 @@
 ):
     count = in_ref.shape[0] // ROWS
     starts = first_rows(count)
+    starts_back = first_rows(count, True)
     pairs = count // 2
     height = pairs * CHANNELS
     for block in range(count):
@@ -163,7 +166,7 @@
         corr = (corr_ref[rows, :] + skip * scaled).astype(NARROW)
         for half in range(2):
             columns = slice(half * LANES, (half + 1) * LANES)
-            first = starts[2 * pair + half]
+            first = starts_back[2 * pair + half]
             out_ref[first : first + CHANNELS, :] = conv[:, columns]
             out_ref[first + CHANNELS : first + EXTRA, :] = corr[:, columns]
     bias = jnp.broadcast_to(jnp.sum(bias, axis=1, keepdims=True), (CHANNELS, LANES))
@@ -173,7 +176,7 @@
     tail = jnp.where(even, bias_high, bias - bias_high)
     for block in range(count):
         rows = jnp.concatenate([lag_ref[block : block + 1, :], tail], axis=0)
-        out_ref[starts[block] + EXTRA : starts[block] + ROWS, :] = rows.astype(NARROW)
+        out_ref[starts_back[block] + EXTRA : starts_back[block] + ROWS, :] = rows.astype(NARROW)
 
 
 def finish_kernel(
@@ -181,7 +184,7 @@
 ):
     per_block = LANES // CHANNELS
     lane = lax.broadcasted_iota(jnp.int32, (1, LANES), 1) // CHANNELS
-    starts = first_rows(filter_out.shape[0])
+    starts = first_rows(filter_out.shape[0], True)
     copies = []
     for piece in range(key_ref.shape[1] // PIECE):
         for block in range(piece * PIECE // LANES, (piece + 1) * PIECE // LANES):
@@ -217,11 +220,11 @@
         copy.wait()
 
 
-def exchange(messages):
+def exchange(messages, back=False):
     count = lax.axis_size("ctx")
     split = messages.reshape(count, ROWS // 2, 2, LANES)
     moved = lax.all_to_all(
-        split, "ctx", split_axis=0, concat_axis=0, tiled=True, axis_index_groups=[listing(count)]
+        split, "ctx", split_axis=0, concat_axis=0, tiled=True, axis_index_groups=[listing(count, back)]
     )
     return moved.reshape(messages.shape)
 
@@ -271,7 +274,7 @@
         compiler_params=grant,
         name="sequence",
     )(skip_bias.reshape(channels // LANES, LANES), moved)
-    back = exchange(results)
+    back = exchange(results, True)
     wide_out = jax.ShapeDtypeStruct((tokens, channels), NARROW)
     grad_query, grad_key, grad_value, grad_filters, grad_bias = pl.pallas_call(
         finish_kernel,

time: 99.7 us -> 99.4 us (level)
  the two profiles are of different devices: /device:TPU:36 before, /device:TPU:68 now
where the time goes in v5:
time: 99.4 us; the launch traced here: 99.2 us
  blocking collectives  90.2 us (91%)
  Pallas kernels  8.25 us (8%)
    all_to_all x2, blocking collectives, exchange(): lax.all_to_all(split, 'ctx', split_axis=0, concat_axis=0, tiled=True, axi...  90.2 us
    pallas_call x1, Pallas kernels, on_device(): pl.pallas_call(sequence_kernel, out_shape=message, scratch_shapes=[pltpu....  4.97 us

profile of v5, /device:TPU:68, one launch (start us, length us, event | category | flops | bytes accessed | tf_op | source)
XLA Modules:
  0.0 99.2 jit_solution(15450802011328027408)
XLA Ops:
  0.6 1.5 %gate.1 = bf16[2176,128]{1,0:T(8,128)(2,1)S(1)} custom-call(bf16[128,1024]{1,0:T(8,128)(2,1)} %query_ref.1, bf16[128,1024]{1,0:T(8,128)(2,1)} %key_ref.3, bf16[128,1024]{1,0:T(8,128)(2,1)} %value_ref.3, bf16[128,1024]{1,0:T(8,128)(2,1)} %grad_ref.3, f32[64,128]{1,0:T(8,128)} %filter_ref.1), custom_call_target="tpu_custom_call" | custom-call | tf_op jit(solution)/shard_map/gate/pallas_call | solution.py:241
  2.2 0.0 copy-start.3
  2.2 49.8 %all_to_all.10 = bf16[64,17,2,128]{3,2,1,0:T(2,128)(2,1)S(1)} all-to-all(bf16[64,17,2,128]{3,2,1,0:T(2,128)(2,1)S(1)} %bitcast.9), channel_id=1, replica_groups={{0,288,64,352,128,416,192,480,256,32,320,96,384,160,448,224,8,296,72,36..., dimensions={0} | all-to-all | bytes 1114112 | tf_op jit(solution)/shard_map/all_to_all | solution.py:226
  52.0 0.0 copy-done.3
  52.0 5.0 %sequence.1 = bf16[2176,128]{1,0:T(8,128)(2,1)S(1)} custom-call(f32[8,128]{1,0:T(8,128)S(1)} %bitcast.10, bf16[2176,128]{1,0:T(8,128)(2,1)S(1)} %bitcast.7), custom_call_target="tpu_custom_call" | custom-call | tf_op jit(solution)/shard_map/sequence/pallas_call | solution.py:261
  56.9 0.0 copy-start
  56.9 0.0 copy-start.1
  57.0 0.0 copy-start.2
  57.0 40.5 %all_to_all.11 = bf16[64,17,2,128]{3,2,1,0:T(2,128)(2,1)S(1)} all-to-all(bf16[64,17,2,128]{3,2,1,0:T(2,128)(2,1)S(1)} %bitcast.8), channel_id=1, replica_groups={{0,416,320,224,128,32,448,352,256,160,64,480,384,288,192,96,8,424,328,2..., dimensions={0} | all-to-all | bytes 1114112 | tf_op jit(solution)/shard_map/all_to_all | solution.py:226
  97.4 0.0 copy-done
  97.4 0.0 copy-done.1
  97.5 0.0 copy-done.2
  97.5 1.7 %finish.1 = (bf16[128,1024]{1,0:T(8,128)(2,1)}, bf16[128,1024]{1,0:T(8,128)(2,1)}, bf16[128,1024]{1,0:T(8,128)(2,1)}, f32[64,128]{1,0:T(8,128)}, f32[8,128]{1,0:T(8,128)}) custom-call(bf16[2176,128]{1,0:T(8,128)(2,1)S(1)} %bitcast.6, bf16[128,1024]{1,0:T(8,128)(2,1)S(1)} %copy-done, bf16[128,1024]{1,0:T(8,128)(2,1)S(1)} %copy-done.1, ...), custom_call_target="tpu_custom_call" | custom-call | tf_op jit(solution)/shard_map/finish/pallas_call | solution.py:279
Async XLA Ops:
  2.2 49.8 %copy-start.3 = (f32[1024]{0:T(1024)S(1)}, f32[1024]{0:T(1024)}, u32[]{:S(2)}) copy-start(f32[1024]{0:T(1024)} %param.11) | copy-start | bytes 12292
  56.9 40.5 %copy-start = (bf16[128,1024]{1,0:T(8,128)(2,1)S(1)}, bf16[128,1024]{1,0:T(8,128)(2,1)}, u32[]{:S(2)}) copy-start(bf16[128,1024]{1,0:T(8,128)(2,1)} %key_ref.3) | copy-start | bytes 786436
  56.9 40.5 %copy-start.1 = (bf16[128,1024]{1,0:T(8,128)(2,1)S(1)}, bf16[128,1024]{1,0:T(8,128)(2,1)}, u32[]{:S(2)}) copy-start(bf16[128,1024]{1,0:T(8,128)(2,1)} %value_ref.3) | copy-start | bytes 786436
  57.0 40.5 %copy-start.2 = (bf16[128,1024]{1,0:T(8,128)(2,1)S(1)}, bf16[128,1024]{1,0:T(8,128)(2,1)}, u32[]{:S(2)}) copy-start(bf16[128,1024]{1,0:T(8,128)(2,1)} %grad_ref.3) | copy-start | bytes 786436

commit v6 on v5

--- a/solution.py
+++ b/solution.py
@@ -132,7 +132,7 @@
         else:
             conv_ref[offset:, :] += conv
             corr_ref[: height - offset, :] += corr
-        depth = min(height, -(-(height - offset) // 256) * 256)
+        depth = min(height, -(-(height - offset) // LANES) * LANES)
         product = jnp.dot(
             turned_ref[:, :depth], scaled_ref[offset : offset + depth, :], preferred_element_type=WIDE
         )

time: 99.4 us -> 99.4 us (level)
  the two profiles are of different devices: /device:TPU:68 before, /device:TPU:66 now
where the time goes in v6:
time: 99.4 us; the launch traced here: 99.2 us
  blocking collectives  90.3 us (91%)
  Pallas kernels  8.19 us (8%)
    all_to_all x2, blocking collectives, exchange(): lax.all_to_all(split, 'ctx', split_axis=0, concat_axis=0, tiled=True, axi...  90.3 us
    pallas_call x1, Pallas kernels, on_device(): pl.pallas_call(sequence_kernel, out_shape=message, scratch_shapes=[pltpu....  4.91 us

profile of v6, /device:TPU:66, one launch (start us, length us, event | category | flops | bytes accessed | tf_op | source)
XLA Modules:
  0.0 99.2 jit_solution(6788422700545125869)
XLA Ops:
  0.6 1.5 %gate.1 = bf16[2176,128]{1,0:T(8,128)(2,1)S(1)} custom-call(bf16[128,1024]{1,0:T(8,128)(2,1)} %query_ref.1, bf16[128,1024]{1,0:T(8,128)(2,1)} %key_ref.3, bf16[128,1024]{1,0:T(8,128)(2,1)} %value_ref.3, bf16[128,1024]{1,0:T(8,128)(2,1)} %grad_ref.3, f32[64,128]{1,0:T(8,128)} %filter_ref.1), custom_call_target="tpu_custom_call" | custom-call | tf_op jit(solution)/shard_map/gate/pallas_call | solution.py:241
  2.2 0.0 copy-start.3
  2.2 49.8 %all_to_all.10 = bf16[64,17,2,128]{3,2,1,0:T(2,128)(2,1)S(1)} all-to-all(bf16[64,17,2,128]{3,2,1,0:T(2,128)(2,1)S(1)} %bitcast.9), channel_id=1, replica_groups={{0,288,64,352,128,416,192,480,256,32,320,96,384,160,448,224,8,296,72,36..., dimensions={0} | all-to-all | bytes 1114112 | tf_op jit(solution)/shard_map/all_to_all | solution.py:226
  52.0 0.0 copy-done.3
  52.0 4.9 %sequence.1 = bf16[2176,128]{1,0:T(8,128)(2,1)S(1)} custom-call(f32[8,128]{1,0:T(8,128)S(1)} %bitcast.10, bf16[2176,128]{1,0:T(8,128)(2,1)S(1)} %bitcast.7), custom_call_target="tpu_custom_call" | custom-call | tf_op jit(solution)/shard_map/sequence/pallas_call | solution.py:261
  56.9 0.0 copy-start
  56.9 0.0 copy-start.1
  56.9 0.0 copy-start.2
  56.9 40.5 %all_to_all.11 = bf16[64,17,2,128]{3,2,1,0:T(2,128)(2,1)S(1)} all-to-all(bf16[64,17,2,128]{3,2,1,0:T(2,128)(2,1)S(1)} %bitcast.8), channel_id=1, replica_groups={{0,416,320,224,128,32,448,352,256,160,64,480,384,288,192,96,8,424,328,2..., dimensions={0} | all-to-all | bytes 1114112 | tf_op jit(solution)/shard_map/all_to_all | solution.py:226
  97.4 0.0 copy-done
  97.4 0.0 copy-done.1
  97.4 0.0 copy-done.2
  97.4 1.7 %finish.1 = (bf16[128,1024]{1,0:T(8,128)(2,1)}, bf16[128,1024]{1,0:T(8,128)(2,1)}, bf16[128,1024]{1,0:T(8,128)(2,1)}, f32[64,128]{1,0:T(8,128)}, f32[8,128]{1,0:T(8,128)}) custom-call(bf16[2176,128]{1,0:T(8,128)(2,1)S(1)} %bitcast.6, bf16[128,1024]{1,0:T(8,128)(2,1)S(1)} %copy-done, bf16[128,1024]{1,0:T(8,128)(2,1)S(1)} %copy-done.1, ...), custom_call_target="tpu_custom_call" | custom-call | tf_op jit(solution)/shard_map/finish/pallas_call | solution.py:279
Async XLA Ops:
  2.2 49.8 %copy-start.3 = (f32[1024]{0:T(1024)S(1)}, f32[1024]{0:T(1024)}, u32[]{:S(2)}) copy-start(f32[1024]{0:T(1024)} %param.11) | copy-start | bytes 12292
  56.9 40.5 %copy-start = (bf16[128,1024]{1,0:T(8,128)(2,1)S(1)}, bf16[128,1024]{1,0:T(8,128)(2,1)}, u32[]{:S(2)}) copy-start(bf16[128,1024]{1,0:T(8,128)(2,1)} %key_ref.3) | copy-start | bytes 786436
  56.9 40.5 %copy-start.1 = (bf16[128,1024]{1,0:T(8,128)(2,1)S(1)}, bf16[128,1024]{1,0:T(8,128)(2,1)}, u32[]{:S(2)}) copy-start(bf16[128,1024]{1,0:T(8,128)(2,1)} %value_ref.3) | copy-start | bytes 786436
  56.9 40.5 %copy-start.2 = (bf16[128,1024]{1,0:T(8,128)(2,1)S(1)}, bf16[128,1024]{1,0:T(8,128)(2,1)}, u32[]{:S(2)}) copy-start(bf16[128,1024]{1,0:T(8,128)(2,1)} %grad_ref.3) | copy-start | bytes 786436
